TPU v7x, 512 devices: a whole 4x4x16 slice. The times are simulated.
512 devices in a mesh: dp: 32 (over y, z_lo), height: 16 (over x, z_hi, core).
Axes of the slice: x: 4, y: 4, z: 16 (z_hi: 2, z_lo: 8; z = z_hi * 8 + z_lo), core: 2. Of those that a mesh axis runs over, the one named last changes fastest.
Arguments:
- frames: bfloat16 [32, 256, 128, 128], P('dp', 'height'), may hold values from -6 to 6
- cotangent: bfloat16 [32, 256, 128, 128], P('dp', 'height'), may hold values from -6 to 6
- w_in: bfloat16 [3, 3, 128, 128], P(None, None, 'dp'), may hold values from -0.1875 to 0.1875
- w_down: bfloat16 [3, 3, 128, 256], P(None, None, 'dp'), may hold values from -0.1875 to 0.1875
- w_up: bfloat16 [3, 3, 256, 128], P(None, None, 'dp'), may hold values from -0.25 to 0.25
Outputs:
- output: bfloat16 [32, 256, 128, 128], P('dp', 'height')
- input_grad: bfloat16 [32, 256, 128, 128], P('dp', 'height')
- grad_in: float32 [3, 3, 128, 128], P(None, None, 'dp', 'height')
- grad_down: float32 [3, 3, 128, 256], P(None, None, 'dp', 'height')
- grad_up: float32 [3, 3, 256, 128], P(None, None, 'dp', 'height')
All inputs are finite; a program needn't handle non-finite values.
Results may differ from a plain program's by a relative error of at most 0.0055.
Values may be sent and summed in bfloat16 or wider, within the bound.
A program may use at most 64 MiB of HBM per device.

v0:
```python
import math

import jax
import jax.numpy as jnp
from jax import lax
from jax.experimental import pallas as pl
from jax.experimental.pallas import tpu as pltpu
from jax.sharding import PartitionSpec as P

F32, BF16 = jnp.float32, jnp.bfloat16
MESH = pl.DeviceIdType.MESH

PACK = 208
DOWN_AT = 48
UP_AT = 128
PIECE = 64
PIECE_STEP = 48
HOPS = (1, -1, 2, -2, 3, -3, 4)


def place():
    d = lax.axis_index("dp")
    h = lax.axis_index("height")
    z = lax.rem(lax.div(h, 2), 2) * 8 + lax.rem(d, 8)
    return lax.div(h, 4), lax.div(d, 8), z, lax.rem(h, 2)


def device(x, y, z, core):
    return (y * 8 + lax.rem(z, 8), x * 4 + lax.div(z, 8) * 2 + core)


def on_ring(position, by, size):
    return lax.rem(position + by + size, size)


def remote(source, target, sends, recvs, slot, where):
    return pltpu.make_async_remote_copy(
        src_ref=source,
        dst_ref=target,
        send_sem=sends.at[slot],
        recv_sem=recvs.at[slot],
        device_id=where,
        device_id_type=MESH,
    )


def meet(partners):
    barrier = pltpu.get_barrier_semaphore()
    for partner in partners:
        pl.semaphore_signal(barrier, inc=1, device_id=partner, device_id_type=MESH)
    pl.semaphore_wait(barrier, len(partners))


def gather_kernel(
    own,
    frames,
    cotangent,
    full,
    frames_above,
    frames_below,
    cotangent_above,
    cotangent_below,
    z_send,
    z_recv,
    y_send,
    y_recv,
    c_send,
    c_recv,
    h_send,
    h_recv,
):
    x, y, z, core = place()
    z_lo = lax.rem(z, 8)
    mine = y * 8 + z_lo
    holder = lax.div(z_lo, 4) == core
    other = device(x, y, z, 1 - core)
    row, band = lax.axis_index("dp"), lax.axis_index("height")
    over, under = (row, on_ring(band, -1, 16)), (row, on_ring(band, 1, 16))
    meet(
        [device(x, y, on_ring(z, by, 16), core) for by in (1, -1, 2, -2, 3, -3, 4, -4)]
        + [device(x, on_ring(y, by, 4), z, core) for by in (1, 2, 3)]
        + [other, over, under]
    )

    def halo(slot, source, rows, target, where):
        return remote(source.at[rows], target, h_send, h_recv, slot, where)

    downward = (
        halo(0, frames, pl.ds(12, 4), frames_above, under),
        halo(1, cotangent, pl.ds(13, 3), cotangent_above, under),
    )
    upward = (
        halo(2, frames, pl.ds(0, 3), frames_below, over),
        halo(3, cotangent, pl.ds(0, 2), cotangent_below, over),
    )
    first, last = band == 0, band == 15

    def unless(condition, action):
        @pl.when(jnp.logical_not(condition))
        def _():
            action()

    def along_z(slot, by):
        return remote(own, full.at[mine], z_send, z_recv, slot, device(x, y, on_ring(z, by, 16), core))

    @pl.when(holder)
    def _():
        for slot, by in enumerate(HOPS):
            along_z(slot, by).start()
        full[mine] = own[...]

    unless(last, lambda: [copy.start() for copy in downward])
    unless(first, lambda: [copy.start() for copy in upward])

    @pl.when(first)
    def _():
        frames_above[...] = jnp.zeros_like(frames_above)
        cotangent_above[...] = jnp.zeros_like(cotangent_above)

    @pl.when(last)
    def _():
        frames_below[...] = jnp.zeros_like(frames_below)
        cotangent_below[...] = jnp.zeros_like(cotangent_below)

    for slot, by in enumerate(HOPS):
        source = lax.rem(on_ring(z, -by, 16), 8)

        @pl.when(lax.div(source, 4) == core)
        def _():
            along_z(slot, by).wait_recv()

    def block(by, half):
        return full.at[pl.ds(on_ring(y, -by, 4) * 8 + half * 4, 4)]

    def along_y(by):
        return remote(block(0, core), block(0, core), y_send, y_recv, by - 1, device(x, on_ring(y, by, 4), z, core))

    def across(by):
        return remote(block(by, core), block(by, core), c_send, c_recv, by, other)

    for by in (1, 3, 2):
        along_y(by).start()
    across(0).start()
    for by in (1, 3, 2):
        along_y(by).wait_recv()
        across(by).start()
    for by in range(4):
        across(by).wait_recv()

    @pl.when(holder)
    def _():
        for slot, by in enumerate(HOPS):
            along_z(slot, by).wait_send()

    for by in (1, 2, 3):
        along_y(by).wait_send()
    for by in range(4):
        across(by).wait_send()
    unless(first, lambda: [copy.wait_recv() for copy in downward])
    unless(last, lambda: [copy.wait_recv() for copy in upward])
    unless(last, lambda: [copy.wait_send() for copy in downward])
    unless(first, lambda: [copy.wait_send() for copy in upward])


def gather(packed, frames, cotangent):
    return pl.pallas_call(
        gather_kernel,
        out_shape=(
            jax.ShapeDtypeStruct((32, PACK, 128), BF16),
            jax.ShapeDtypeStruct((4, 128, 128), BF16),
            jax.ShapeDtypeStruct((3, 128, 128), BF16),
            jax.ShapeDtypeStruct((3, 128, 128), BF16),
            jax.ShapeDtypeStruct((2, 128, 128), BF16),
        ),
        in_specs=[pl.BlockSpec(memory_space=pltpu.VMEM)] + [pl.BlockSpec(memory_space=pl.ANY)] * 2,
        out_specs=(pl.BlockSpec(memory_space=pltpu.VMEM),) * 5,
        scratch_shapes=[
            pltpu.SemaphoreType.DMA((7,)),
            pltpu.SemaphoreType.DMA((7,)),
            pltpu.SemaphoreType.DMA((3,)),
            pltpu.SemaphoreType.DMA((3,)),
            pltpu.SemaphoreType.DMA((4,)),
            pltpu.SemaphoreType.DMA((4,)),
            pltpu.SemaphoreType.DMA((4,)),
            pltpu.SemaphoreType.DMA((4,)),
        ],
        compiler_params=pltpu.CompilerParams(
            collective_id=0, has_side_effects=True, vmem_limit_bytes=32 << 20
        ),
    )(packed, frames, cotangent)


def spread_columns(rows, first, wide, stacked, slots):
    count = rows.shape[0]
    wide[pl.ds(first, count), 8:136] = rows[...].astype(F32)
    for row in range(first, first + count):
        target = stacked.at[row] if len(stacked.shape) == 3 else stacked.at[row // 2, row % 2]
        for slot in range(slots):
            target[:, slot * 128 : slot * 128 + 128] = wide[row, pl.ds(7 + slot, 64, stride=2), :].astype(BF16)


def matmul(left, right):
    return lax.dot_general(left, right, (((1,), (0,)), ((), ())), preferred_element_type=F32)


def matmul_t(left, right):
    return lax.dot_general(left, right, (((1,), (1,)), ((), ())), preferred_element_type=F32)


def flat(cells):
    return cells.reshape(cells.shape[0] * cells.shape[1], cells.shape[2])


def shuffle(taps, channels, pitch, transposed):
    shards = 16 // channels
    dims = (shards * pitch, taps * 16) if transposed else (taps * 16, shards * pitch)
    row = lax.broadcasted_iota(jnp.int32, dims, 1 if transposed else 0)
    column = lax.broadcasted_iota(jnp.int32, dims, 0 if transposed else 1)
    bits = channels.bit_length() - 1
    wanted = ((row & 15) >> bits) * pitch + (row >> 4) * channels + (row & (channels - 1))
    return (column == wanted).astype(F32).astype(BF16)


def unpack_weights(full, win, wdn, wup):
    order = shuffle(9, 4, 48, False)
    for group in range(8):
        rows = matmul(order, full[4 * group : 4 * group + 4, 0:DOWN_AT].reshape(192, 128)).astype(BF16)
        win[:, 16 * group : 16 * group + 16] = rows.reshape(9, 16, 128)
    order = shuffle(18, 4, 80, False)
    for group in range(8):
        rows = matmul(order, full[4 * group : 4 * group + 4, DOWN_AT:UP_AT].reshape(320, 128)).astype(BF16)
        wdn[:, 16 * group : 16 * group + 16, 0:128] = rows[0:144].reshape(9, 16, 128)
        wdn[:, 16 * group : 16 * group + 16, 128:256] = rows[144:288].reshape(9, 16, 128)
    order = shuffle(9, 8, 80, False)
    for group in range(16):
        rows = matmul(order, full[2 * group : 2 * group + 2, UP_AT:PACK].reshape(160, 128)).astype(BF16)
        wup[:, 16 * group : 16 * group + 16] = rows.reshape(9, 16, 128)


def pack_sums(parts, sin, sdn, sup):
    order = shuffle(9, 4, 48, True)
    for group in range(8):
        rows = matmul(order, sin[:, 16 * group : 16 * group + 16].reshape(144, 128)).astype(BF16)
        parts[4 * group : 4 * group + 4, 0:DOWN_AT] = rows.reshape(4, 48, 128)
    order = shuffle(18, 4, 80, True)
    for group in range(8):
        halves = [sdn[:, 16 * group : 16 * group + 16, at : at + 128].reshape(144, 128) for at in (0, 128)]
        rows = matmul(order, jnp.concatenate(halves, axis=0)).astype(BF16)
        parts[4 * group : 4 * group + 4, DOWN_AT:UP_AT] = rows.reshape(4, 80, 128)
    order = shuffle(9, 8, 80, True)
    for group in range(16):
        rows = matmul(order, sup[:, 16 * group : 16 * group + 16].reshape(144, 128)).astype(BF16)
        parts[2 * group : 2 * group + 2, UP_AT:PACK] = rows.reshape(2, 80, 128)


def stack_weights(win, wdn, wup, fine, down, up, back_fine, back_down, back_up):
    blank = jnp.zeros((128, 128), BF16)
    for j in range(3):
        for slot in range(4):
            at = slice(slot * 128, slot * 128 + 128)
            fine[j, at, 0:128] = win[3 * j + slot] if slot < 3 else blank
            fine[j, at, 128:256] = win[3 * j + slot - 1] if slot > 0 else blank
            back_fine[j, 0:128, at] = win[3 * (2 - j) + 2 - slot] if slot < 3 else blank
            back_fine[j, 128:256, at] = win[3 * (2 - j) + 3 - slot] if slot > 0 else blank
        for slot in range(3):
            at = slice(slot * 128, slot * 128 + 128)
            down[j, at, :] = wdn[3 * j + slot]
            back_up[j, :, at] = wup[3 * (2 - j) + 2 - slot]
        up[j, 0:256, 0:128] = wup[3 * j + 1]
        up[j, 0:256, 128:256] = wup[3 * j]
        up[j, 256:512, 0:128] = jnp.zeros((256, 128), BF16)
        up[j, 256:512, 128:256] = wup[3 * j + 2]
        back_down[j, 0:128, 0:256] = wdn[3 * j + 1]
        back_down[j, 0:128, 256:512] = jnp.zeros((128, 256), BF16)
        back_down[j, 128:256, 0:256] = wdn[3 * j + 2]
        back_down[j, 128:256, 256:512] = wdn[3 * j]


def sigmoid(value):
    return 1.0 / (1.0 + jnp.exp(-value))


def compute_kernel(
    frames,
    frames_above,
    frames_below,
    cotangent,
    cotangent_above,
    cotangent_below,
    full,
    output,
    input_grad,
    parts,
    wide,
    fx,
    h3,
    c3,
    slopes,
    shifted,
    shifted_wide,
    coarse2,
    grad2,
    gx,
    mixed,
    win,
    wdn,
    wup,
    fine,
    down,
    up,
    back_fine,
    back_down,
    back_up,
):
    band = lax.axis_index("height")
    top, bottom = band == 0, band == lax.axis_size("height") - 1
    unpack_weights(full, win, wdn, wup)
    stack_weights(win, wdn, wup, fine, down, up, back_fine, back_down, back_up)

    wide[:, 0:8] = jnp.zeros((23, 8, 128), F32)
    wide[:, 136:144] = jnp.zeros((23, 8, 128), F32)
    shifted[:, 0:8] = jnp.zeros((9, 8, 128), F32)
    shifted[:, 72:80] = jnp.zeros((9, 8, 128), F32)
    shifted_wide[:, 64:72] = jnp.zeros((10, 8, 256), F32)
    spread_columns(frames_above, 0, wide, fx, 4)
    spread_columns(frames, 4, wide, fx, 4)
    spread_columns(frames_below, 20, wide, fx, 4)

    for first in (0, 7, 14):
        pre = sum(matmul(flat(fx[first + j : first + j + 7]), fine[j]) for j in range(3))
        gate = sigmoid(pre)
        hidden = (pre * gate).reshape(7, 64, 256)
        slope = (gate * (1.0 + pre * (1.0 - gate))).reshape(7, 64, 256)
        shifted[0:7, 8:72] = hidden[:, :, 128:256]
        before = shifted[0:7, 7:71].astype(BF16)
        hidden = hidden.astype(BF16)
        for row in range(7):
            i = first + row
            h3[i // 2, i % 2, :, 0:128] = before[row]
            h3[i // 2, i % 2, :, 128:384] = hidden[row]
            if 2 <= i < 20:
                slopes[i - 2] = slope[row]

    @pl.when(top)
    def _():
        for i in range(3):
            h3[i // 2, i % 2] = jnp.zeros((64, 384), BF16)

    @pl.when(bottom)
    def _():
        for i in (19, 20):
            h3[i // 2, i % 2] = jnp.zeros((64, 384), BF16)

    spread_columns(cotangent_above, 0, wide, c3, 3)
    spread_columns(cotangent, 3, wide, c3, 3)
    spread_columns(cotangent_below, 19, wide, c3, 3)

    views = ((0, 0), (0, 1), (1, 0))
    pre = sum(matmul(flat(h3[a : a + 10, b]), down[j]) for j, (a, b) in enumerate(views))
    gate = sigmoid(pre)
    coarse = (pre * gate).reshape(10, 64, 256)
    shifted_wide[:, 0:64] = coarse
    coarse2[:, :, 0:256] = coarse.astype(BF16)
    coarse2[:, :, 256:512] = shifted_wide[:, 1:65].astype(BF16)
    back = sum(matmul_t(flat(c3[a : a + 10, b]), back_up[j]) for j, (a, b) in enumerate(views))
    grad = (back * (gate * (1.0 + pre * (1.0 - gate)))).reshape(10, 64, 256)
    shifted_wide[:, 0:64] = grad
    grad2[:, :, 0:256] = grad.astype(BF16)
    grad2[:, :, 256:512] = shifted_wide[:, 1:65].astype(BF16)

    @pl.when(top)
    def _():
        grad2[0] = jnp.zeros((64, 512), BF16)

    @pl.when(bottom)
    def _():
        coarse2[9] = jnp.zeros((64, 512), BF16)
        grad2[9] = jnp.zeros((64, 512), BF16)

    def mix(row, cells):
        mixed[row, pl.ds(0, 64, stride=2), :] = cells[:, 0:128]
        mixed[row, pl.ds(1, 64, stride=2), :] = cells[:, 128:256]

    even = matmul(flat(coarse2[1:9]), up[1])
    odd = matmul(flat(coarse2[1:9]), up[0]) + matmul(flat(coarse2[2:10]), up[2])
    for t in range(8):
        mix(2 * t, even[64 * t : 64 * t + 64])
        mix(2 * t + 1, odd[64 * t : 64 * t + 64])
    output[...] = (frames[...].astype(F32) + mixed[...]).astype(BF16)

    grad_even = matmul_t(flat(grad2[1:10]), back_down[1]).reshape(9, 64, 256)
    grad_odd = (
        matmul_t(flat(grad2[0:9]), back_down[2]) + matmul_t(flat(grad2[1:10]), back_down[0])
    ).reshape(9, 64, 256)
    for start, rows in ((0, grad_odd), (1, grad_even)):
        rows = jnp.concatenate([rows[m : m + 1] * slopes[start + 2 * m][None] for m in range(9)], axis=0)
        ready = rows.astype(BF16)
        shifted[:, 8:72] = rows[:, :, 128:256]
        before = shifted[:, 7:71].astype(BF16)
        shifted[:, 8:72] = rows[:, :, 0:128]
        after = shifted[:, 9:73].astype(BF16)
        for m in range(9):
            gx[start + 2 * m, :, 0:128] = before[m]
            gx[start + 2 * m, :, 128:384] = ready[m]
            gx[start + 2 * m, :, 384:512] = after[m]

    @pl.when(top)
    def _():
        gx[0] = jnp.zeros((64, 512), BF16)

    @pl.when(bottom)
    def _():
        gx[17] = jnp.zeros((64, 512), BF16)

    for first in (0, 8):
        back = sum(matmul_t(flat(gx[first + j : first + j + 8]), back_fine[j]) for j in range(3))
        for row in range(8):
            mix(first + row, back[64 * row : 64 * row + 64])
    input_grad[...] = (cotangent[...].astype(F32) + mixed[...]).astype(BF16)

    turned = flat(coarse2[1:9, :, 0:256]).T
    for j, (a, b) in enumerate(views):
        found = matmul(turned, flat(c3[a + 1 : a + 9, b]))
        for slot in range(3):
            wup[3 * (2 - j) + 2 - slot] = found[:, slot * 128 : slot * 128 + 128].astype(BF16)
    turned = flat(grad2[1:9, :, 0:256]).T
    for j, (a, b) in enumerate(views):
        found = matmul(turned, flat(h3[a + 1 : a + 9, b]))
        for slot in range(3):
            wdn[3 * j + slot] = found[:, slot * 128 : slot * 128 + 128].T.astype(BF16)
    turned = flat(gx[1:17, :, 128:384]).T
    for j in range(3):
        found = matmul(turned, flat(fx[3 + j : 19 + j]))
        for l in range(3):
            both = found[0:128, l * 128 : l * 128 + 128] + found[128:256, (l + 1) * 128 : (l + 2) * 128]
            win[3 * j + l] = both.T.astype(BF16)
    pack_sums(parts, win, wdn, wup)


def compute(frames, frames_above, frames_below, cotangent, cotangent_above, cotangent_below, full):
    vmem = pltpu.VMEM
    whole = pl.BlockSpec(memory_space=vmem)
    return pl.pallas_call(
        compute_kernel,
        out_shape=(
            jax.ShapeDtypeStruct((16, 128, 128), BF16),
            jax.ShapeDtypeStruct((16, 128, 128), BF16),
            jax.ShapeDtypeStruct((32, PACK, 128), BF16),
        ),
        in_specs=[whole] * 7,
        out_specs=(whole,) * 3,
        scratch_shapes=[
            vmem((23, 144, 128), F32),
            vmem((23, 64, 512), BF16),
            vmem((11, 2, 64, 384), BF16),
            vmem((11, 2, 64, 384), BF16),
            vmem((18, 64, 256), F32),
            vmem((9, 80, 128), F32),
            vmem((10, 72, 256), F32),
            vmem((10, 64, 512), BF16),
            vmem((10, 64, 512), BF16),
            vmem((18, 64, 512), BF16),
            vmem((16, 128, 128), F32),
            vmem((9, 128, 128), BF16),
            vmem((9, 128, 256), BF16),
            vmem((9, 256, 128), BF16),
            vmem((3, 512, 256), BF16),
            vmem((3, 384, 256), BF16),
            vmem((3, 512, 256), BF16),
            vmem((3, 256, 512), BF16),
            vmem((3, 256, 512), BF16),
            vmem((3, 256, 384), BF16),
        ],
        compiler_params=pltpu.CompilerParams(vmem_limit_bytes=48 << 20),
    )(frames, frames_above, frames_below, cotangent, cotangent_above, cotangent_below, full)


def reduce_kernel(
    parts,
    total,
    from_core,
    to_y,
    from_y,
    sums,
    to_z,
    from_z,
    column,
    from_x,
    piece,
    from_far,
    done,
    all_pieces,
    c_send,
    c_recv,
    y_send,
    y_recv,
    z_send,
    z_recv,
    x_send,
    x_recv,
    f_send,
    f_recv,
    a_send,
    a_recv,
    b_send,
    b_recv,
):
    x, y, z, core = place()
    z_lo = lax.rem(z, 8)
    holder = lax.div(z_lo, 4) == core
    other = device(x, y, z, 1 - core)
    far = on_ring(z, 8, 16)
    meet(
        [device(x, y, on_ring(z, by, 16), core) for by in (1, -1, 2, -2, 3, -3, 4, -4, 8)]
        + [device(x, on_ring(y, by, 4), z, core) for by in (1, 2, 3)]
        + [device(on_ring(x, by, 4), y, z, core) for by in (1, 2, 3)]
        + [device(on_ring(x, by, 4), y, z, 1 - core) for by in (0, 1, 2, 3)]
    )

    def rows_of(by, half):
        return pl.ds(on_ring(y, by, 4) * 8 + half * 4, 4)

    def across(by):
        return remote(parts.at[rows_of(by, 1 - core)], from_core.at[by], c_send, c_recv, by, other)

    def along_y(by):
        return remote(to_y.at[by - 1], from_y.at[by - 1], y_send, y_recv, by - 1, device(x, on_ring(y, by, 4), z, core))

    for by in (1, 3, 2, 0):
        across(by).start()
    for by in (1, 3, 2):
        across(by).wait_recv()
        to_y[by - 1] = (
            parts[rows_of(by, core)].astype(F32) + from_core[by].astype(F32)
        ).astype(BF16)
        along_y(by).start()
    across(0).wait_recv()
    sums[...] = parts[rows_of(0, core)].astype(F32) + from_core[0].astype(F32)
    for by in (1, 3, 2):
        along_y(by).wait_recv()
        sums[...] += from_y[by - 1].astype(F32)
    to_z[...] = sums[...].astype(BF16)

    def along_z(slot, by):
        where = on_ring(z, by, 16)
        return remote(
            to_z.at[lax.rem(where, 4)], from_z.at[slot], z_send, z_recv, slot, device(x, y, where, core)
        )

    for slot, by in enumerate(HOPS):

        @pl.when(lax.div(lax.rem(on_ring(z, by, 16), 8), 4) == core)
        def _():
            along_z(slot, by).start()

    def along_x(by):
        where = on_ring(x, by, 4)
        return remote(
            column.at[pl.ds(where * PIECE_STEP, PIECE)],
            from_x.at[by - 1],
            x_send,
            x_recv,
            by - 1,
            device(where, y, z, core),
        )

    def to_far():
        return remote(piece, from_far, f_send, f_recv, 0, device(x, y, far, core))

    def spread(by):
        return remote(done, all_pieces.at[x], a_send, a_recv, by, device(on_ring(x, by, 4), y, z, core))

    def spread_other(by):
        return remote(done, all_pieces.at[x], b_send, b_recv, by, device(on_ring(x, by, 4), y, z, 1 - core))

    @pl.when(holder)
    def _():
        column[...] = sums[lax.rem(z_lo, 4)]
        for slot, by in enumerate(HOPS):
            along_z(slot, by).wait_recv()
            column[...] += from_z[slot].astype(F32)
        for by in (1, 3, 2):
            along_x(by).start()
        piece[...] = column[pl.ds(x * PIECE_STEP, PIECE)]
        for by in (1, 3, 2):
            along_x(by).wait_recv()
            piece[...] += from_x[by - 1]
        to_far().start()
        to_far().wait_recv()
        done[...] = piece[...] + from_far[...]
        for by in (2, 1, 3):
            spread(by).start()
        for by in (2, 1, 3, 0):
            spread_other(by).start()
        all_pieces[x] = done[...]
        for by in (1, 2, 3):
            spread(by).wait_recv()
        for by in (1, 2, 3):
            along_x(by).wait_send()
        to_far().wait_send()
        for by in (1, 2, 3):
            spread(by).wait_send()
        for by in range(4):
            spread_other(by).wait_send()

    @pl.when(jnp.logical_not(holder))
    def _():
        for by in range(4):
            spread_other(by).wait_recv()

    for source in range(4):
        total[pl.ds(source * PIECE_STEP, PIECE)] = all_pieces[source]
    for by in range(4):
        across(by).wait_send()
    for by in (1, 2, 3):
        along_y(by).wait_send()
    for slot, by in enumerate(HOPS):

        @pl.when(lax.div(lax.rem(on_ring(z, by, 16), 8), 4) == core)
        def _():
            along_z(slot, by).wait_send()


def reduce_over_all(parts):
    dma = pltpu.SemaphoreType.DMA
    counts = (4, 3, 7, 3, 1, 4, 4)
    return pl.pallas_call(
        reduce_kernel,
        out_shape=jax.ShapeDtypeStruct((PACK, 128), F32),
        in_specs=[pl.BlockSpec(memory_space=pltpu.VMEM)],
        out_specs=pl.BlockSpec(memory_space=pltpu.VMEM),
        scratch_shapes=[
            pltpu.VMEM((4, 4, PACK, 128), BF16),
            pltpu.VMEM((3, 4, PACK, 128), BF16),
            pltpu.VMEM((3, 4, PACK, 128), BF16),
            pltpu.VMEM((4, PACK, 128), F32),
            pltpu.VMEM((4, PACK, 128), BF16),
            pltpu.VMEM((7, PACK, 128), BF16),
            pltpu.VMEM((PACK, 128), F32),
            pltpu.VMEM((3, PIECE, 128), F32),
            pltpu.VMEM((PIECE, 128), F32),
            pltpu.VMEM((PIECE, 128), F32),
            pltpu.VMEM((PIECE, 128), F32),
            pltpu.VMEM((4, PIECE, 128), F32),
        ]
        + [dma((count,)) for count in counts for _ in range(2)],
        compiler_params=pltpu.CompilerParams(
            collective_id=1, has_side_effects=True, vmem_limit_bytes=32 << 20
        ),
    )(parts)


def pack(w_in, w_down, w_up):
    def rows(kernel, size):
        return jnp.pad(kernel, ((0, 0), (0, size - kernel.shape[1]), (0, 0)))

    count = w_in.shape[0]
    halves = w_down.reshape(count, 36, 2, 128).transpose(0, 2, 1, 3).reshape(count, 72, 128)
    return jnp.concatenate(
        [
            rows(w_in.reshape(count, 36, 128), DOWN_AT),
            rows(halves, UP_AT - DOWN_AT),
            rows(w_up.reshape(count, 72, 128), PACK - UP_AT),
        ],
        axis=1,
    )


def unpack(packed):
    count = packed.shape[0]
    halves = packed[:, DOWN_AT : DOWN_AT + 72].reshape(count, 2, 36, 128).transpose(0, 2, 1, 3)
    return (
        packed[:, :36].reshape(count, 9, 4, 128),
        halves.reshape(count, 9, 4, 256),
        packed[:, UP_AT : UP_AT + 72].reshape(count, 9, 8, 128),
    )


def on_device(frames, cotangent, w_in, w_down, w_up):
    frames, cotangent = frames[0], cotangent[0]
    full, *halos = gather(pack(w_in[None], w_down[None], w_up[None])[0], frames, cotangent)
    output, input_grad, parts = compute(frames, *halos[:2], cotangent, *halos[2:], full)
    summed = reduce_over_all(parts)
    height = lax.axis_size("height")
    pixel_count = lax.axis_size("dp") * height * frames.shape[0] * frames.shape[1]
    factor = 1.0 / math.sqrt(pixel_count)
    index = lax.axis_index("height")
    shares = []
    for part in unpack(summed[None] * factor):
        width = part.shape[3] // height
        share = lax.dynamic_slice_in_dim(part[0], index * width, width, axis=2)
        shares.append(share.reshape(3, 3, part.shape[2], width))
    return (output[None], input_grad[None], *shares)


def solution(mesh):
    in_specs = (
        P("dp", "height", None, None),
        P("dp", "height", None, None),
        P(None, None, "dp", None),
        P(None, None, "dp", None),
        P(None, None, "dp", None),
    )
    out_specs = (
        P("dp", "height", None, None),
        P("dp", "height", None, None),
        P(None, None, "dp", "height"),
        P(None, None, "dp", "height"),
        P(None, None, "dp", "height"),
    )
    return jax.shard_map(
        on_device, mesh=mesh, in_specs=in_specs, out_specs=out_specs, check_vma=False
    )
```

profile of v0, /device:TPU:1, one launch (start us, length us, event | category | flops | bytes accessed | tf_op | source)
XLA Modules:
  0.0 111.3 jit_solution(15908983193051991757)
XLA Ops:
  0.6 0.7 reshape_broadcast_in_dim.10
  1.4 0.7 reshape_broadcast_in_dim.9
  2.1 0.7 fusion.6.own
  2.8 0.0 copy-start
  2.8 1.0 copy-done
  3.9 0.0 copy-start.2
  3.9 1.0 copy-done.2
  4.9 44.1 %shard_map.92 = (bf16[32,208,128]{2,1,0:T(8,128)(2,1)S(1)}, bf16[4,128,128]{2,1,0:T(8,128)(2,1)S(1)}, bf16[3,128,128]{2,1,0:T(8,128)(2,1)S(1)}, bf16[3,128,128]{2,1,0:T(8,128)(2,1)S(1)}, bf16[2,128,128]{2,1,0:T(8,128)(2,1)S(1)}) custom-call(bf16[208,128]{1,0:T(8,128)(2,1)S(1)} %fusion.6.own, bf16[16,128,128]{2,1,0:T(8,128)(2,1)S(1)} %bitcast.20, ...), custom_call_target="tpu_custom_call" | custom-call | tf_op jit(solution)/shard_map/pallas_call | solution.py:166
  49.0 0.0 copy-start.1
  49.0 1.0 copy-done.1
  50.1 0.0 copy-start.3
  50.1 1.0 copy-done.3
  51.1 10.9 %shard_map.93 = (bf16[16,128,128]{2,1,0:T(8,128)(2,1)}, bf16[16,128,128]{2,1,0:T(8,128)(2,1)}, bf16[32,208,128]{2,1,0:T(8,128)(2,1)S(1)}) custom-call(bf16[16,128,128]{2,1,0:T(8,128)(2,1)S(1)} %bitcast.21, bf16[4,128,128]{2,1,0:T(8,128)(2,1)S(1)} %get-tuple-element.13.frames_above, bf16[3,128,128]{2,1,0:T(8,128)(2,1)S(1)} %get-tuple-element.14.frames_below, ...), custom_call_target="tpu_custom_call" | custom-call | tf_op jit(solution)/shard_map/pallas_call | solution.py:443
  62.0 47.1 %shard_map.94 = f32[208,128]{1,0:T(8,128)S(1)} custom-call(bf16[32,208,128]{2,1,0:T(8,128)(2,1)S(1)} %get-tuple-element.20.parts), custom_call_target="tpu_custom_call" | custom-call | tf_op jit(solution)/shard_map/pallas_call | solution.py:627
  109.2 0.7 constant_dynamic-slice_fusion
  109.9 0.7 constant_dynamic-slice_fusion.1
  110.6 0.7 constant_dynamic-slice_fusion.2
  (8 shorter events, 0.1 us)
Async XLA Ops:
  2.8 1.0 copy-start
  3.9 1.0 copy-start.2
  49.0 1.0 copy-start.1
  50.1 1.0 copy-start.3
where the time goes:
time: 112 us; the launch traced here: 111 us
  Pallas kernels  102 us (91%)
  local copies, waits for them, and re-layouts  7.79 us (7%)
    pallas_call x1, Pallas kernels, reduce_over_all(): pl.pallas_call(reduce_kernel, out_shape=jax.ShapeDtypeStruct((PACK, 128),...  47.1 us
    pallas_call x1, Pallas kernels, gather(): pl.pallas_call(gather_kernel, out_shape=(jax.ShapeDtypeStruct((32, PACK,...  44.1 us
    pallas_call x1, Pallas kernels, compute(): pl.pallas_call(compute_kernel, out_shape=(jax.ShapeDtypeStruct((16, 128,...  10.9 us
    unnamed x8, local copies, waits for them, and re-layouts  4.16 us

commit v1 on v0

--- a/solution.py
+++ b/solution.py
@@ -76,11 +76,6 @@
     other = device(x, y, z, 1 - core)
     row, band = lax.axis_index("dp"), lax.axis_index("height")
     over, under = (row, on_ring(band, -1, 16)), (row, on_ring(band, 1, 16))
-    meet(
-        [device(x, y, on_ring(z, by, 16), core) for by in (1, -1, 2, -2, 3, -3, 4, -4)]
-        + [device(x, on_ring(y, by, 4), z, core) for by in (1, 2, 3)]
-        + [other, over, under]
-    )
 
     def halo(slot, source, rows, target, where):
         return remote(source.at[rows], target, h_send, h_recv, slot, where)
@@ -160,34 +155,6 @@
     unless(last, lambda: [copy.wait_recv() for copy in upward])
     unless(last, lambda: [copy.wait_send() for copy in downward])
     unless(first, lambda: [copy.wait_send() for copy in upward])
-
-
-def gather(packed, frames, cotangent):
-    return pl.pallas_call(
-        gather_kernel,
-        out_shape=(
-            jax.ShapeDtypeStruct((32, PACK, 128), BF16),
-            jax.ShapeDtypeStruct((4, 128, 128), BF16),
-            jax.ShapeDtypeStruct((3, 128, 128), BF16),
-            jax.ShapeDtypeStruct((3, 128, 128), BF16),
-            jax.ShapeDtypeStruct((2, 128, 128), BF16),
-        ),
-        in_specs=[pl.BlockSpec(memory_space=pltpu.VMEM)] + [pl.BlockSpec(memory_space=pl.ANY)] * 2,
-        out_specs=(pl.BlockSpec(memory_space=pltpu.VMEM),) * 5,
-        scratch_shapes=[
-            pltpu.SemaphoreType.DMA((7,)),
-            pltpu.SemaphoreType.DMA((7,)),
-            pltpu.SemaphoreType.DMA((3,)),
-            pltpu.SemaphoreType.DMA((3,)),
-            pltpu.SemaphoreType.DMA((4,)),
-            pltpu.SemaphoreType.DMA((4,)),
-            pltpu.SemaphoreType.DMA((4,)),
-            pltpu.SemaphoreType.DMA((4,)),
-        ],
-        compiler_params=pltpu.CompilerParams(
-            collective_id=0, has_side_effects=True, vmem_limit_bytes=32 << 20
-        ),
-    )(packed, frames, cotangent)
 
 
 def spread_columns(rows, first, wide, stacked, slots):
@@ -437,44 +404,6 @@
     pack_sums(parts, win, wdn, wup)
 
 
-def compute(frames, frames_above, frames_below, cotangent, cotangent_above, cotangent_below, full):
-    vmem = pltpu.VMEM
-    whole = pl.BlockSpec(memory_space=vmem)
-    return pl.pallas_call(
-        compute_kernel,
-        out_shape=(
-            jax.ShapeDtypeStruct((16, 128, 128), BF16),
-            jax.ShapeDtypeStruct((16, 128, 128), BF16),
-            jax.ShapeDtypeStruct((32, PACK, 128), BF16),
-        ),
-        in_specs=[whole] * 7,
-        out_specs=(whole,) * 3,
-        scratch_shapes=[
-            vmem((23, 144, 128), F32),
-            vmem((23, 64, 512), BF16),
-            vmem((11, 2, 64, 384), BF16),
-            vmem((11, 2, 64, 384), BF16),
-            vmem((18, 64, 256), F32),
-            vmem((9, 80, 128), F32),
-            vmem((10, 72, 256), F32),
-            vmem((10, 64, 512), BF16),
-            vmem((10, 64, 512), BF16),
-            vmem((18, 64, 512), BF16),
-            vmem((16, 128, 128), F32),
-            vmem((9, 128, 128), BF16),
-            vmem((9, 128, 256), BF16),
-            vmem((9, 256, 128), BF16),
-            vmem((3, 512, 256), BF16),
-            vmem((3, 384, 256), BF16),
-            vmem((3, 512, 256), BF16),
-            vmem((3, 256, 512), BF16),
-            vmem((3, 256, 512), BF16),
-            vmem((3, 256, 384), BF16),
-        ],
-        compiler_params=pltpu.CompilerParams(vmem_limit_bytes=48 << 20),
-    )(frames, frames_above, frames_below, cotangent, cotangent_above, cotangent_below, full)
-
-
 def reduce_kernel(
     parts,
     total,
@@ -510,12 +439,6 @@
     holder = lax.div(z_lo, 4) == core
     other = device(x, y, z, 1 - core)
     far = on_ring(z, 8, 16)
-    meet(
-        [device(x, y, on_ring(z, by, 16), core) for by in (1, -1, 2, -2, 3, -3, 4, -4, 8)]
-        + [device(x, on_ring(y, by, 4), z, core) for by in (1, 2, 3)]
-        + [device(on_ring(x, by, 4), y, z, core) for by in (1, 2, 3)]
-        + [device(on_ring(x, by, 4), y, z, 1 - core) for by in (0, 1, 2, 3)]
-    )
 
     def rows_of(by, half):
         return pl.ds(on_ring(y, by, 4) * 8 + half * 4, 4)
@@ -621,33 +544,102 @@
             along_z(slot, by).wait_send()
 
 
-def reduce_over_all(parts):
-    dma = pltpu.SemaphoreType.DMA
-    counts = (4, 3, 7, 3, 1, 4, 4)
+def whole_kernel(
+    own,
+    frames,
+    cotangent,
+    output,
+    input_grad,
+    total,
+    full,
+    frames_above,
+    frames_below,
+    cotangent_above,
+    cotangent_below,
+    parts,
+    *scratch,
+):
+    x, y, z, core = place()
+    row, band = lax.axis_index("dp"), lax.axis_index("height")
+    meet(
+        [device(x, y, on_ring(z, by, 16), core) for by in (1, -1, 2, -2, 3, -3, 4, -4, 8)]
+        + [device(x, on_ring(y, by, 4), z, core) for by in (1, 2, 3)]
+        + [device(on_ring(x, by, 4), y, z, core) for by in (1, 2, 3)]
+        + [device(on_ring(x, by, 4), y, z, 1 - core) for by in (0, 1, 2, 3)]
+        + [(row, on_ring(band, -1, 16)), (row, on_ring(band, 1, 16))]
+    )
+    halos = (frames_above, frames_below, cotangent_above, cotangent_below)
+    for_gather, for_compute, for_reduce = scratch[:8], scratch[8:28], scratch[28:]
+    gather_kernel(own, frames, cotangent, full, *halos, *for_gather)
+    inputs = (frames, *halos[:2], cotangent, *halos[2:], full)
+    compute_kernel(*inputs, output, input_grad, parts, *for_compute)
+    reduce_kernel(parts, total, *for_reduce)
+
+
+def whole(packed, frames, cotangent):
+    vmem, dma = pltpu.VMEM, pltpu.SemaphoreType.DMA
+    spec = pl.BlockSpec(memory_space=vmem)
+    gather_counts = (7, 3, 4, 4)
+    reduce_counts = (4, 3, 7, 3, 1, 4, 4)
     return pl.pallas_call(
-        reduce_kernel,
-        out_shape=jax.ShapeDtypeStruct((PACK, 128), F32),
-        in_specs=[pl.BlockSpec(memory_space=pltpu.VMEM)],
-        out_specs=pl.BlockSpec(memory_space=pltpu.VMEM),
+        whole_kernel,
+        out_shape=(
+            jax.ShapeDtypeStruct((16, 128, 128), BF16),
+            jax.ShapeDtypeStruct((16, 128, 128), BF16),
+            jax.ShapeDtypeStruct((PACK, 128), F32),
+        ),
+        in_specs=[spec] * 3,
+        out_specs=(spec,) * 3,
         scratch_shapes=[
-            pltpu.VMEM((4, 4, PACK, 128), BF16),
-            pltpu.VMEM((3, 4, PACK, 128), BF16),
-            pltpu.VMEM((3, 4, PACK, 128), BF16),
-            pltpu.VMEM((4, PACK, 128), F32),
-            pltpu.VMEM((4, PACK, 128), BF16),
-            pltpu.VMEM((7, PACK, 128), BF16),
-            pltpu.VMEM((PACK, 128), F32),
-            pltpu.VMEM((3, PIECE, 128), F32),
-            pltpu.VMEM((PIECE, 128), F32),
-            pltpu.VMEM((PIECE, 128), F32),
-            pltpu.VMEM((PIECE, 128), F32),
-            pltpu.VMEM((4, PIECE, 128), F32),
+            vmem((32, PACK, 128), BF16),
+            vmem((4, 128, 128), BF16),
+            vmem((3, 128, 128), BF16),
+            vmem((3, 128, 128), BF16),
+            vmem((2, 128, 128), BF16),
+            vmem((32, PACK, 128), BF16),
         ]
-        + [dma((count,)) for count in counts for _ in range(2)],
+        + [dma((count,)) for count in gather_counts for _ in range(2)]
+        + [
+            vmem((23, 144, 128), F32),
+            vmem((23, 64, 512), BF16),
+            vmem((11, 2, 64, 384), BF16),
+            vmem((11, 2, 64, 384), BF16),
+            vmem((18, 64, 256), F32),
+            vmem((9, 80, 128), F32),
+            vmem((10, 72, 256), F32),
+            vmem((10, 64, 512), BF16),
+            vmem((10, 64, 512), BF16),
+            vmem((18, 64, 512), BF16),
+            vmem((16, 128, 128), F32),
+            vmem((9, 128, 128), BF16),
+            vmem((9, 128, 256), BF16),
+            vmem((9, 256, 128), BF16),
+            vmem((3, 512, 256), BF16),
+            vmem((3, 384, 256), BF16),
+            vmem((3, 512, 256), BF16),
+            vmem((3, 256, 512), BF16),
+            vmem((3, 256, 512), BF16),
+            vmem((3, 256, 384), BF16),
+        ]
+        + [
+            vmem((4, 4, PACK, 128), BF16),
+            vmem((3, 4, PACK, 128), BF16),
+            vmem((3, 4, PACK, 128), BF16),
+            vmem((4, PACK, 128), F32),
+            vmem((4, PACK, 128), BF16),
+            vmem((7, PACK, 128), BF16),
+            vmem((PACK, 128), F32),
+            vmem((3, PIECE, 128), F32),
+            vmem((PIECE, 128), F32),
+            vmem((PIECE, 128), F32),
+            vmem((PIECE, 128), F32),
+            vmem((4, PIECE, 128), F32),
+        ]
+        + [dma((count,)) for count in reduce_counts for _ in range(2)],
         compiler_params=pltpu.CompilerParams(
-            collective_id=1, has_side_effects=True, vmem_limit_bytes=32 << 20
+            collective_id=0, has_side_effects=True, vmem_limit_bytes=56 << 20
         ),
-    )(parts)
+    )(packed, frames, cotangent)
 
 
 def pack(w_in, w_down, w_up):
@@ -678,9 +670,8 @@
 
 def on_device(frames, cotangent, w_in, w_down, w_up):
     frames, cotangent = frames[0], cotangent[0]
-    full, *halos = gather(pack(w_in[None], w_down[None], w_up[None])[0], frames, cotangent)
-    output, input_grad, parts = compute(frames, *halos[:2], cotangent, *halos[2:], full)
-    summed = reduce_over_all(parts)
+    packed = pack(w_in[None], w_down[None], w_up[None])[0]
+    output, input_grad, summed = whole(packed, frames, cotangent)
     height = lax.axis_size("height")
     pixel_count = lax.axis_size("dp") * height * frames.shape[0] * frames.shape[1]
     factor = 1.0 / math.sqrt(pixel_count)

time: 112 us -> 106 us (0.946)
  Pallas kernels: 102 us -> 96.9 us
  local copies, waits for them, and re-layouts: 7.79 us -> 6.34 us
    pallas_call x3 -> x1, Pallas kernels: 102 us -> 96.9 us  [whole(): pl.pallas_call(whole_kernel, out_shape=(jax.ShapeDtypeStruct((16, 128, 12...]
    unnamed x8 -> x10, local copies, waits for them, and re-layouts: 4.16 us -> 3.41 us
where the time goes in v1:
time: 106 us
  Pallas kernels  96.9 us (91%)
  local copies, waits for them, and re-layouts  6.34 us (6%)
  other arithmetic  1.59 us (2%)
    pallas_call x1, Pallas kernels, whole(): pl.pallas_call(whole_kernel, out_shape=(jax.ShapeDtypeStruct((16, 128, 12...  96.9 us
    unnamed x10, local copies, waits for them, and re-layouts  3.41 us

profile of v1, /device:TPU:1, one launch (start us, length us, event | category | flops | bytes accessed | tf_op | source)
XLA Modules:
  0.0 105.5 jit_solution(2285980649881502838)
XLA Ops:
  0.6 0.7 reshape_broadcast_in_dim.10
  1.4 0.0 copy-start.3
  1.4 0.7 copy-done.3
  2.1 0.0 copy-start.2
  2.1 0.7 copy-done.2
  2.8 0.6 fusion.6.own
  3.4 96.9 %shard_map.92 = (bf16[16,128,128]{2,1,0:T(8,128)(2,1)}, bf16[16,128,128]{2,1,0:T(8,128)(2,1)}, f32[208,128]{1,0:T(8,128)}) custom-call(bf16[208,128]{1,0:T(8,128)(2,1)} %fusion.6.own, bf16[16,128,128]{2,1,0:T(8,128)(2,1)} %bitcast.20, bf16[16,128,128]{2,1,0:T(8,128)(2,1)} %bitcast.21), custom_call_target="tpu_custom_call" | custom-call | tf_op jit(solution)/shard_map/pallas_call | solution.py:584
  100.4 0.0 copy-start.1
  100.4 1.0 multiply_bitcast_fusion
  101.4 0.7 constant_dynamic-slice_fusion
  102.1 0.7 constant_dynamic-slice_fusion.1
  102.8 0.7 constant_dynamic-slice_fusion.2
  103.5 0.0 copy-done.1
  103.5 0.0 copy-start
  103.5 0.8 copy.17
  104.3 0.4 copy-done
  104.8 0.8 copy.18
  (8 shorter events, 0.1 us)
Async XLA Ops:
  1.4 0.7 copy-start.3
  2.1 0.7 copy-start.2
  100.4 3.2 %copy-start.1 = (bf16[16,128,128]{2,1,0:T(8,128)(2,1)S(1)}, bf16[16,128,128]{2,1,0:T(8,128)(2,1)}, u32[]{:S(2)}) copy-start(bf16[16,128,128]{2,1,0:T(8,128)(2,1)} %get-tuple-element.8) | copy-start | bytes 1572868
  103.5 1.2 %copy-start = (bf16[16,128,128]{2,1,0:T(8,128)(2,1)S(1)}, bf16[16,128,128]{2,1,0:T(8,128)(2,1)}, u32[]{:S(2)}) copy-start(bf16[16,128,128]{2,1,0:T(8,128)(2,1)} %get-tuple-element.9) | copy-start | bytes 1572868
